TPU v7x, 32 devices: a whole 2x2x4 slice. The times are simulated.
32 devices in a mesh: dp: 8 (over z, y), owner: 4 (over x, core).
Axes of the slice: x: 2, y: 2, z: 4, core: 2. Of those that a mesh axis runs over, the one named last changes fastest.
Arguments:
- tokens: bfloat16 [1024, 4096], P('dp'), may hold values from -6 to 6
- act_basis: bfloat16 [2, 4096, 4096], P(None, 'dp', 'owner'), may hold values from -0.09375 to 0.09375
- grad_basis: bfloat16 [2, 8192, 8192], P(None, 'owner', 'dp'), may hold values from -0.0625 to 0.0625
- grads: bfloat16 [2, 1024, 8192], P(None, 'dp', 'owner'), may hold values from -6 to 6
- expert_ids: int32 [1024, 2], P('dp'), may hold values from 0 to 7, all different within a row; in each aligned block of 128 rows (0 to 127, 128 to 255, ...) at most 64 rows name the same one
Outputs:
- corrected: float32 [2, 8192, 4096], P(None, 'dp', 'owner')
Inputs may be any that keep to these rules, and one draw needn't show every extreme that they name: `expert_ids`: among the 128 rows of one device no expert is named by more than 64 rows, a bound that some block reaches; the two experts of a row differ.
All inputs are finite; a program needn't handle non-finite values.
Results may differ from a plain program's by a relative error of at most 0.0013.
Values may be sent and summed in bfloat16 or wider, within the bound.
A program may use at most 128 MiB of HBM per device.

v0:
```python
import jax
import jax.numpy as jnp
from jax import lax
from jax.sharding import PartitionSpec as P


def compact(expert_ids, tokens, grads, capacity):
    slot_order = jnp.arange(capacity, dtype=jnp.int32)[:, None]
    choosers = []
    for expert in range(grads.shape[0]):
        routed = jnp.any(expert_ids == expert, axis=1)
        slot_index = jnp.cumsum(routed.astype(jnp.int32)) - 1
        chosen = jnp.logical_and(routed[None, :], slot_index[None, :] == slot_order)
        choosers.append(chosen.astype(jnp.bfloat16))
    chooser = jnp.stack(choosers)
    picked_act = jnp.einsum(
        "ect,td->ecd", chooser, tokens, preferred_element_type=jnp.float32
    ).astype(jnp.bfloat16)
    picked_grad = jnp.einsum(
        "ect,etf->ecf", chooser, grads, preferred_element_type=jnp.float32
    ).astype(jnp.bfloat16)
    return (picked_act, picked_grad)


def correct(picked_act, picked_grad, act_basis, grad_basis, token_total):
    projected = jnp.einsum(
        "ecn,ena->eca",
        picked_act,
        lax.all_gather(act_basis, "dp", axis=1, tiled=True),
        preferred_element_type=jnp.float32,
    )
    act_all = lax.all_gather(projected.astype(jnp.bfloat16), "dp", axis=1, tiled=True)
    act_sq = jnp.square(act_all.astype(jnp.float32)).astype(jnp.bfloat16)
    grad_part = jnp.einsum(
        "erf,efk->erk",
        lax.all_gather(picked_grad, "dp", axis=1, tiled=True),
        grad_basis,
        preferred_element_type=jnp.float32,
    )
    grad_all = lax.psum(grad_part, "owner")
    grad_sq = jnp.square(grad_all).astype(jnp.bfloat16)
    return (
        jnp.einsum("erk,era->eka", grad_sq, act_sq, preferred_element_type=jnp.float32)
        / token_total
    )


def per_device(tokens, act_basis, grad_basis, grads, expert_ids):
    tok_rows = tokens.shape[0]
    capacity = tok_rows // 2
    token_total = tok_rows * lax.axis_size("dp")
    picked_act, picked_grad = compact(expert_ids, tokens, grads, capacity)
    results = []
    for expert in range(grads.shape[0]):
        results.append(
            correct(
                picked_act[expert : expert + 1],
                picked_grad[expert : expert + 1],
                act_basis[expert : expert + 1],
                grad_basis[expert : expert + 1],
                token_total,
            )
        )
    return jnp.concatenate(results, axis=0)


def solution(mesh):
    placed = (
        P("dp", None),
        P(None, "dp", "owner"),
        P(None, "owner", "dp"),
        P(None, "dp", "owner"),
        P("dp", None),
    )
    return jax.shard_map(
        per_device, mesh=mesh, in_specs=placed, out_specs=P(None, "dp", "owner"), check_vma=False
    )
```

profile of v0, /device:TPU:15, one launch (start us, length us, event | category | flops | bytes accessed | tf_op | source)
XLA Modules:
  0.0 543.1 jit_solution(12613459593378850933)
XLA Ops:
  6.5 0.0 copy-start
  6.5 0.0 copy-start.2
  6.5 0.0 all-gather.9.cloned.1.call-start
  6.5 0.8 compare_reduce_fusion.1
  7.4 0.1 copy.9
  7.5 0.2 reduce-window.17
  7.7 0.1 add_reduce_fusion
  7.8 0.1 copy.8
  7.9 0.2 reduce-window.16
  8.1 0.1 add_reduce_fusion.1
  8.2 1.5 convolution_convert_fusion.1
  9.8 0.9 fusion.38
  10.6 0.0 all-gather.9.cloned.1.call-update
  10.6 0.0 all-gather.13.cloned.1.call-start
  10.7 0.7 all-gather.13.cloned.1.call-update
  11.4 0.0 all-gather.15.cloned.1.call-start
  11.4 0.0 copy-done.2
  11.4 1.5 fusion.37
  13.0 0.0 all-gather.15.cloned.1.call-update
  13.0 0.0 all-gather.11.cloned.1.call-start
  13.0 0.5 all-gather.11.cloned.1.call-update
  13.6 0.0 all-reduce.3.cloned.1.call-start
  13.6 45.8 %all-gather.9.cloned.1.call-done = bf16[1,512,2048]{2,1,0:T(8,128)(2,1)} async-done(((bf16[1,64,2048]{2,1,0:T(8,128)(2,1)}), bf16[1,512,2048]{2,1,0:T(8,128)(2,1)}) %all-gather.9.cloned.1.call-update) | async-done | bytes 2097168 | tf_op jit(solution)/shard_map/all_gather | solution.py:36
  59.4 6.5 %fusion.12 = f32[1,512,1024]{2,1,0:T(8,128)} fusion(bf16[2,2048,1024]{2,1,0:T(8,128)(2,1)} %param.7, bf16[1,512,2048]{2,1,0:T(8,128)(2,1)} %all-gather.9.cloned.1.call-done), kind=kOutput, calls=%fused_computation.21 | convolution fusion | flops 2147483648 | bytes 8388608 | tf_op jit(solution)/shard_map/erf,efk->erk/dot_general | solution.py:34
  65.9 43.5 %all-gather.13.cloned.1.call-done = bf16[1,512,2048]{2,1,0:T(8,128)(2,1)} async-done(((bf16[1,64,2048]{2,1,0:T(8,128)(2,1)}), bf16[1,512,2048]{2,1,0:T(8,128)(2,1)}) %all-gather.13.cloned.1.call-update) | async-done | bytes 2097168 | tf_op jit(solution)/shard_map/all_gather | solution.py:36
  109.3 6.5 %fusion.17 = f32[1,512,1024]{2,1,0:T(8,128)} fusion(bf16[2,2048,1024]{2,1,0:T(8,128)(2,1)} %param.7, bf16[1,512,2048]{2,1,0:T(8,128)(2,1)} %all-gather.13.cloned.1.call-done), kind=kOutput, calls=%fused_computation.22 | convolution fusion | flops 2147483648 | bytes 8388608 | tf_op jit(solution)/shard_map/erf,efk->erk/dot_general | solution.py:34
  115.8 0.0 all-reduce.3.cloned.1.call-update
  115.8 0.0 all-gather.19.cloned.1.call-start
  115.9 0.0 copy-done
  115.9 0.4 convolution_convert_fusion
  116.3 117.2 %all-gather.15.cloned.1.call-done = bf16[1,4096,1024]{2,1,0:T(8,128)(2,1)} async-done(((bf16[1,512,1024]{2,1,0:T(8,128)(2,1)}), bf16[1,4096,1024]{2,1,0:T(8,128)(2,1)}) %all-gather.15.cloned.1.call-update) | async-done | bytes 8388624 | tf_op jit(solution)/shard_map/all_gather | solution.py:29
  233.5 5.6 %fusion.25 = bf16[64,1024]{1,0:T(8,128)(2,1)} fusion(bf16[1,4096,1024]{2,1,0:T(8,128)(2,1)} %all-gather.15.cloned.1.call-done, bf16[2,64,4096]{2,1,0:T(8,128)(2,1)S(1)} %convolution_convert_fusion), kind=kOutput, calls=%fused_computation.24 | convolution fusion | flops 536936448 | bytes 9043968 | tf_op jit(solution)/shard_map/ecn,ena->eca/dot_general | solution.py:26
  239.1 0.0 all-gather.19.cloned.1.call-update
  239.2 0.0 all-gather.17.cloned.1.call-start
  239.2 119.4 %all-gather.11.cloned.1.call-done = bf16[1,4096,1024]{2,1,0:T(8,128)(2,1)} async-done(((bf16[1,512,1024]{2,1,0:T(8,128)(2,1)}), bf16[1,4096,1024]{2,1,0:T(8,128)(2,1)}) %all-gather.11.cloned.1.call-update) | async-done | bytes 8388624 | tf_op jit(solution)/shard_map/all_gather | solution.py:29
  358.7 5.6 %fusion.22 = bf16[64,1024]{1,0:T(8,128)(2,1)} fusion(bf16[1,4096,1024]{2,1,0:T(8,128)(2,1)} %all-gather.11.cloned.1.call-done, bf16[2,64,4096]{2,1,0:T(8,128)(2,1)S(1)} %convolution_convert_fusion), kind=kOutput, calls=%fused_computation.23 | convolution fusion | flops 536936448 | bytes 9043968 | tf_op jit(solution)/shard_map/ecn,ena->eca/dot_general | solution.py:26
  364.3 0.0 all-gather.17.cloned.1.call-update
  364.3 83.2 %all-reduce.3.cloned.1.call-done = (f32[1,512,1024]{2,1,0:T(8,128)}, f32[1,512,1024]{2,1,0:T(8,128)}) async-done(((f32[1,512,1024]{2,1,0:T(8,128)}, f32[1,512,1024]{2,1,0:T(8,128)}), (f32[1,512,1024]{2,1,0:T(8,128)}, f32[1,512,1024]{2,1,0:T(8,128)})) %all-reduce.3.cloned.1.call-update) | async-done | bytes 4194320 | tf_op jit(solution)/shard_map/psum | solution.py:40
  447.5 40.6 %all-gather.19.cloned.1.call-done = bf16[512,1024]{1,0:T(8,128)(2,1)} async-done(((bf16[64,1024]{1,0:T(8,128)(2,1)}), bf16[512,1024]{1,0:T(8,128)(2,1)}) %all-gather.19.cloned.1.call-update) | async-done | bytes 1048592 | tf_op jit(solution)/shard_map/all_gather | solution.py:32
  488.0 0.0 copy-start.3
  488.0 5.3 multiply_bitcast_fusion
  493.4 36.0 %all-gather.17.cloned.1.call-done = bf16[512,1024]{1,0:T(8,128)(2,1)} async-done(((bf16[64,1024]{1,0:T(8,128)(2,1)}), bf16[512,1024]{1,0:T(8,128)(2,1)}) %all-gather.17.cloned.1.call-update) | async-done | bytes 1048592 | tf_op jit(solution)/shard_map/all_gather | solution.py:32
  529.3 0.0 copy-done.3
  529.3 0.0 copy-start.1
  529.3 2.7 multiply_bitcast_fusion.1
  532.0 0.0 copy-done.1
  532.0 4.2 pad_maximum_fusion
  (3 shorter events, 0.0 us)
Async XLA Ops:
  6.5 109.4 %copy-start = (bf16[128,4096]{1,0:T(8,128)(2,1)S(1)}, bf16[128,4096]{1,0:T(8,128)(2,1)}, u32[]{:S(2)}) copy-start(bf16[128,4096]{1,0:T(8,128)(2,1)} %param.5) | copy-start | bytes 3145732
  6.5 4.9 copy-start.2
  6.5 52.9 %all-gather.9.cloned.1.call-start = ((), (), s32[]{:S(2)}) async-start(), calls=%async_computation | async-start | bytes 2359296 | tf_op jit(solution)/shard_map/all_gather | solution.py:36
  10.6 98.7 %all-gather.13.cloned.1.call-start = ((), (), s32[]{:S(2)}) async-start(), calls=%async_computation.2 | async-start | bytes 2359296 | tf_op jit(solution)/shard_map/all_gather | solution.py:36
  11.4 222.1 %all-gather.15.cloned.1.call-start = ((), (), s32[]{:S(2)}) async-start(), calls=%async_computation.3 | async-start | bytes 9437184 | tf_op jit(solution)/shard_map/all_gather | solution.py:29
  13.0 345.7 %all-gather.11.cloned.1.call-start = ((), (), s32[]{:S(2)}) async-start(), calls=%async_computation.1 | async-start | bytes 9437184 | tf_op jit(solution)/shard_map/all_gather | solution.py:29
  13.6 433.9 %all-reduce.3.cloned.1.call-start = ((), (), s32[]{:S(2)}) async-start(), calls=%async_computation.6 | async-start | bytes 8388608 | tf_op jit(solution)/shard_map/psum | solution.py:40
  115.8 372.2 %all-gather.19.cloned.1.call-start = ((), (), s32[]{:S(2)}) async-start(), calls=%async_computation.5 | async-start | bytes 1179648 | tf_op jit(solution)/shard_map/all_gather | solution.py:32
  239.2 290.2 %all-gather.17.cloned.1.call-start = ((), (), s32[]{:S(2)}) async-start(), calls=%async_computation.4 | async-start | bytes 1179648 | tf_op jit(solution)/shard_map/all_gather | solution.py:32
  488.0 41.3 %copy-start.3 = (f32[1,512,1024]{2,1,0:T(8,128)S(1)}, f32[1,512,1024]{2,1,0:T(8,128)}, u32[]{:S(2)}) copy-start(f32[1,512,1024]{2,1,0:T(8,128)} %get-tuple-element.8) | copy-start | bytes 6291460
  529.3 2.7 copy-start.1
Sparse Core Ops, SparseCore 0:
  10.8 48.5 all-gather.8
  61.5 47.7 all-gather.12
  111.5 122.0 all-gather.14
  235.5 123.1 all-gather.10
  360.9 86.4 all-reduce.2
  449.7 38.3 all-gather.18
  490.4 38.8 all-gather.16
where the time goes:
time: 547 us; the launch traced here: 543 us
  waiting for transfers between devices  487 us (89%)
  matrix products  34.1 us (6%)
  between operations  13.6 us (2%)
  other arithmetic  5.68 us (1%)
    all_gather x2, waiting for transfers between devices, correct(): lax.all_gather(act_basis, 'dp', axis=1, tiled=True)  237 us
    all_gather x2, waiting for transfers between devices, correct(): lax.all_gather(picked_grad, 'dp', axis=1, tiled=True)  89.2 us
    psum x1, waiting for transfers between devices, correct(): grad_all = lax.psum(grad_part, 'owner')  83.2 us
    all_gather x2, waiting for transfers between devices, correct(): lax.all_gather(projected.astype(jnp.bfloat16), 'dp', axis=1, tiled=True)  76.5 us
    dot_general x2, matrix products, correct(): jnp.einsum('erf,efk->erk', lax.all_gather(picked_grad, 'dp', axis=1, tile...  12.9 us
    dot_general x2, matrix products, correct(): jnp.einsum('ecn,ena->eca', picked_act, lax.all_gather(act_basis, 'dp', ax...  11.2 us
  transfers between devices with their start and end apart: 7, of which 7 were waited for; matrix products, arithmetic and copies ran while one was open for 6% of the time, Pallas kernels for 0%

commit v1 on v0

v1 whole, which is shorter than its diff:
```python
import jax
import jax.numpy as jnp
from jax import lax
from jax.sharding import PartitionSpec as P


def compact(expert_ids, tokens, grads, capacity):
    slot_order = jnp.arange(capacity, dtype=jnp.int32)[:, None]
    choosers = []
    for expert in range(grads.shape[0]):
        routed = jnp.any(expert_ids == expert, axis=1)
        slot_index = jnp.cumsum(routed.astype(jnp.int32)) - 1
        chosen = jnp.logical_and(routed[None, :], slot_index[None, :] == slot_order)
        choosers.append(chosen.astype(jnp.bfloat16))
    chooser = jnp.stack(choosers)
    picked_act = jnp.einsum(
        "ect,td->ecd", chooser, tokens, preferred_element_type=jnp.float32
    ).astype(jnp.bfloat16)
    picked_grad = jnp.einsum(
        "ect,etf->ecf", chooser, grads, preferred_element_type=jnp.float32
    ).astype(jnp.bfloat16)
    return (picked_act, picked_grad)


def per_device(tokens, act_basis, grad_basis, grads, expert_ids):
    tok_rows = tokens.shape[0]
    capacity = tok_rows // 2
    token_total = tok_rows * lax.axis_size("dp")
    picked_act, picked_grad = compact(expert_ids, tokens, grads, capacity)
    grad_rows = lax.all_gather(picked_grad, "dp", axis=1, tiled=True)
    act_rows = lax.all_to_all(picked_act, "dp", split_axis=2, concat_axis=1, tiled=True)
    act_part = jnp.einsum("ern,ena->era", act_rows, act_basis, preferred_element_type=jnp.float32)
    act_own = lax.psum_scatter(act_part, "dp", scatter_dimension=1, tiled=True).astype(jnp.bfloat16)
    act_all = lax.all_gather(act_own, "dp", axis=1, tiled=True)
    act_sq = jnp.square(act_all.astype(jnp.float32)).astype(jnp.bfloat16)
    grad_part = jnp.einsum("erf,efk->erk", grad_rows, grad_basis, preferred_element_type=jnp.float32)
    grad_own = lax.psum_scatter(grad_part, "owner", scatter_dimension=1, tiled=True)
    grad_sq = lax.all_gather(jnp.square(grad_own).astype(jnp.bfloat16), "owner", axis=1, tiled=True)
    return (
        jnp.einsum("erk,era->eka", grad_sq, act_sq, preferred_element_type=jnp.float32)
        / token_total
    )


def solution(mesh):
    placed = (
        P("dp", None),
        P(None, "dp", "owner"),
        P(None, "owner", "dp"),
        P(None, "dp", "owner"),
        P("dp", None),
    )
    return jax.shard_map(
        per_device, mesh=mesh, in_specs=placed, out_specs=P(None, "dp", "owner"), check_vma=False
    )
```

time: 547 us -> 330 us (0.60)
  waiting for transfers between devices: 487 us -> 224 us
  blocking collectives: 0 us -> 41.6 us
  local copies, waits for them, and re-layouts: 2.62 us -> 16.4 us
  matrix products: 34.1 us -> 26.4 us
    all_gather x6 -> x3, waiting for transfers between devices: 402 us -> 98.6 us  [the longest x1 48.3 us: per_device(): act_all = lax.all_gather(act_own, 'dp', axis=1, tiled=True)]
    reduce_scatter x0 -> x2, waiting for transfers between devices: none -> 126 us  [the longest x1 81.4 us: per_device(): lax.psum_scatter(act_part, 'dp', scatter_dimension=1, tiled=True)]
    psum x1 -> x0, waiting for transfers between devices: 83.2 us -> none  [correct(): grad_all = lax.psum(grad_part, 'owner')]
    all_to_all x0 -> x1, blocking collectives: none -> 41.6 us  [per_device(): lax.all_to_all(picked_act, 'dp', split_axis=2, concat_axis=1, tiled=True)]
    dot_general x6 -> x3, matrix products: 32.2 us -> 22.4 us  [the longest x1 11.2 us: per_device(): jnp.einsum('erf,efk->erk', grad_rows, grad_basis, preferred_element_type=...]
    unnamed x8 -> x4, local copies, waits for them, and re-layouts: 0.02 us -> 7.71 us
  transfers between devices with their start and end apart: 7 -> 5, of which waited for: 7 -> 5; matrix products, arithmetic and copies ran while one was open for 6% -> 11% of each run, Pallas kernels for 0% -> 0%
where the time goes in v1:
time: 330 us; the launch traced here: 327 us
  waiting for transfers between devices  224 us (68%)
  blocking collectives  41.6 us (13%)
  matrix products  26.4 us (8%)
  local copies, waits for them, and re-layouts  16.4 us (5%)
  between operations  13.2 us (4%)
  other arithmetic  5.3 us (2%)
    reduce_scatter x1, waiting for transfers between devices, per_device(): lax.psum_scatter(act_part, 'dp', scatter_dimension=1, tiled=True)  81.4 us
    all_gather x1, waiting for transfers between devices, per_device(): act_all = lax.all_gather(act_own, 'dp', axis=1, tiled=True)  48.3 us
    reduce_scatter x1, waiting for transfers between devices, per_device(): lax.psum_scatter(grad_part, 'owner', scatter_dimension=1, tiled=True)  44.2 us
    all_to_all x1, blocking collectives, per_device(): lax.all_to_all(picked_act, 'dp', split_axis=2, concat_axis=1, tiled=True)  41.6 us
    all_gather x1, waiting for transfers between devices, per_device(): grad_rows = lax.all_gather(picked_grad, 'dp', axis=1, tiled=True)  26.5 us
    all_gather x1, waiting for transfers between devices, per_device(): lax.all_gather(jnp.square(grad_own).astype(jnp.bfloat16), 'owner', axis=1...  23.8 us
    dot_general x1, matrix products, per_device(): jnp.einsum('erf,efk->erk', grad_rows, grad_basis, preferred_element_type=...  11.2 us
    dot_general x1, matrix products, per_device(): jnp.einsum('erk,era->eka', grad_sq, act_sq, preferred_element_type=jnp.fl...  8 us
  transfers between devices with their start and end apart: 5, of which 5 were waited for; matrix products, arithmetic and copies ran while one was open for 11% of the time, Pallas kernels for 0%

profile of v1, /device:TPU:15, one launch (start us, length us, event | category | flops | bytes accessed | tf_op | source)
XLA Modules:
  0.0 327.5 jit_solution(857930729796068012)
XLA Ops:
  6.5 0.0 copy-start
  6.5 0.0 all-gather.4.cloned.1.call-start
  6.5 0.8 compare_reduce_fusion.1
  7.4 0.1 copy.16
  7.5 0.2 reduce-window.17
  7.7 0.1 add_reduce_fusion
  7.8 0.1 copy.15
  7.9 0.2 reduce-window.16
  8.1 0.1 add_reduce_fusion.1
  8.2 2.4 convolution_convert_fusion.1
  10.6 0.0 all-gather.4.cloned.1.call-update
  10.6 0.0 reduce-scatter.5.cloned.1.call-start
  10.7 1.7 convolution_convert_fusion
  12.4 3.9 %copy.17 = bf16[2,64,4096]{1,0,2:T(2,128)(2,1)} copy(bf16[2,64,4096]{2,1,0:T(8,128)(2,1)S(1)} %convolution_convert_fusion) | data formatting | bytes 2097152 | tf_op jit(solution)/shard_map/convert_element_type | solution.py:18
  16.2 3.4 %reshape.185 = bf16[8,2,32768]{2,1,0:T(2,128)(2,1)S(1)} reshape(bf16[4096,2,64]{2,1,0:T(2,128)(2,1)} %bitcast.20) | data formatting | bytes 2097152
  19.6 41.6 %all_to_all.18 = bf16[8,2,32768]{2,1,0:T(2,128)(2,1)} all-to-all(bf16[8,2,32768]{2,1,0:T(2,128)(2,1)S(1)} %reshape.185), channel_id=1, replica_groups=mesh['dp'=8,'owner'=4] {'dp'}, dimensions={0} | all-to-all | bytes 2097152 | tf_op jit(solution)/shard_map/all_to_all | solution.py:31
  61.2 4.3 %reshape.186 = bf16[4096,2,64]{2,1,0:T(2,128)(2,1)} reshape(bf16[8,2,32768]{2,1,0:T(2,128)(2,1)} %all_to_all.18) | data formatting | bytes 2097152
  65.6 4.6 %copy.23 = bf16[2,64,8,512]{3,1,2,0:T(8,128)(2,1)S(1)} copy(bf16[2,64,8,512]{1,0,3,2:T(2,128)(2,1)} %bitcast.21) | data formatting | bytes 2097152 | tf_op jit(solution)/shard_map/all_to_all | solution.py:31
  70.2 0.0 copy-done
  70.2 3.2 fusion.6
  73.4 0.0 reduce-scatter.5.cloned.1.call-update
  73.4 0.0 reduce-scatter.3.cloned.1.call-start
  73.5 26.5 %all-gather.4.cloned.1.call-done = bf16[2,512,2048]{2,1,0:T(8,128)(2,1)} async-done(((bf16[2,64,2048]{2,1,0:T(8,128)(2,1)}), bf16[2,512,2048]{2,1,0:T(8,128)(2,1)}) %all-gather.4.cloned.1.call-update) | async-done | bytes 4194320 | tf_op jit(solution)/shard_map/all_gather | solution.py:30
  100.0 11.2 %fusion.5 = f32[2,512,1024]{2,1,0:T(8,128)} fusion(bf16[2,512,2048]{2,1,0:T(8,128)(2,1)} %all-gather.4.cloned.1.call-done, bf16[2,2048,1024]{2,1,0:T(8,128)(2,1)} %param.7), kind=kOutput, calls=%fused_computation.19 | convolution fusion | flops 4294967296 | bytes 16777216 | tf_op jit(solution)/shard_map/erf,efk->erk/dot_general | solution.py:36
  111.2 0.0 reduce-scatter.3.cloned.1.call-update
  111.2 0.0 all-gather.8.cloned.1.call-start
  111.3 81.4 %reduce-scatter.5.cloned.1.call-done = f32[2,64,1024]{2,1,0:T(8,128)} async-done(((f32[2,512,1024]{2,1,0:T(8,128)}), f32[2,64,1024]{2,1,0:T(8,128)}) %reduce-scatter.5.cloned.1.call-update) | async-done | bytes 524304 | tf_op jit(solution)/shard_map/reduce_scatter | solution.py:33
  192.6 1.8 convert_element_type.71
  194.4 0.0 all-gather.8.cloned.1.call-update
  194.4 0.0 all-gather.6.cloned.1.call-start
  194.5 44.2 %reduce-scatter.3.cloned.1.call-done = f32[2,128,1024]{2,1,0:T(8,128)} async-done(((f32[2,512,1024]{2,1,0:T(8,128)}), f32[2,128,1024]{2,1,0:T(8,128)}) %reduce-scatter.3.cloned.1.call-update) | async-done | bytes 1048592 | tf_op jit(solution)/shard_map/reduce_scatter | solution.py:37
  238.7 2.1 multiply_convert_fusion.2
  240.8 0.0 all-gather.6.cloned.1.call-update
  240.8 48.3 %all-gather.8.cloned.1.call-done = bf16[2,512,1024]{2,1,0:T(8,128)(2,1)} async-done(((bf16[2,64,1024]{2,1,0:T(8,128)(2,1)}), bf16[2,512,1024]{2,1,0:T(8,128)(2,1)}) %all-gather.8.cloned.1.call-update) | async-done | bytes 2097168 | tf_op jit(solution)/shard_map/all_gather | solution.py:34
  289.2 23.8 %all-gather.6.cloned.1.call-done = bf16[2,512,1024]{2,1,0:T(8,128)(2,1)} async-done(((bf16[2,128,1024]{2,1,0:T(8,128)(2,1)}), bf16[2,512,1024]{2,1,0:T(8,128)(2,1)}) %all-gather.6.cloned.1.call-update) | async-done | bytes 2097168 | tf_op jit(solution)/shard_map/all_gather | solution.py:38
  312.9 8.0 %broadcast_multiply_fusion = f32[2,1024,1024]{2,1,0:T(8,128)} fusion(bf16[2,512,1024]{2,1,0:T(8,128)(2,1)} %all-gather.6.cloned.1.call-done, bf16[2,512,1024]{2,1,0:T(8,128)(2,1)} %all-gather.8.cloned.1.call-done), kind=kOutput, calls=%fused_computation.1 | convolution fusion | flops 2152726528 | bytes 12582912 | tf_op jit(solution)/shard_map/erk,era->eka/dot_general | solution.py:40
  (3 shorter events, 0.0 us)
Async XLA Ops:
  6.5 63.6 %copy-start = (bf16[2,512,1024]{2,1,0:T(8,128)(2,1)S(1)}, bf16[2,512,1024]{2,1,0:T(8,128)(2,1)}, u32[]{:S(2)}) copy-start(bf16[2,512,1024]{2,1,0:T(8,128)(2,1)} %param.6) | copy-start | bytes 6291460
  6.5 93.5 %all-gather.4.cloned.1.call-start = ((), (), s32[]{:S(2)}) async-start(), calls=%async_computation.3 | async-start | bytes 4718592 | tf_op jit(solution)/shard_map/all_gather | solution.py:30
  10.6 182.0 %reduce-scatter.5.cloned.1.call-start = ((), (), s32[]{:S(2)}) async-start(), calls=%async_computation.6 | async-start | bytes 4718592 | tf_op jit(solution)/shard_map/reduce_scatter | solution.py:33
  73.4 165.2 %reduce-scatter.3.cloned.1.call-start = ((), (), s32[]{:S(2)}) async-start(), calls=%async_computation.4 | async-start | bytes 5242880 | tf_op jit(solution)/shard_map/reduce_scatter | solution.py:37
  111.2 177.9 %all-gather.8.cloned.1.call-start = ((), (), s32[]{:S(2)}) async-start(), calls=%async_computation.7 | async-start | bytes 2359296 | tf_op jit(solution)/shard_map/all_gather | solution.py:34
  194.4 118.5 %all-gather.6.cloned.1.call-start = ((), (), s32[]{:S(2)}) async-start(), calls=%async_computation.5 | async-start | bytes 2621440 | tf_op jit(solution)/shard_map/all_gather | solution.py:38
Sparse Core Ops, SparseCore 0:
  10.8 89.1 all-gather.3
  103.6 88.9 reduce-scatter.4
  195.3 43.3 reduce-scatter.2
  240.7 48.3 all-gather.7
  290.6 22.3 all-gather.5

commit v2 on v1

v2 whole, which is shorter than its diff:
```python
import functools

import jax
import jax.numpy as jnp
from jax import lax
from jax.experimental import pallas as pl
from jax.experimental.pallas import tpu as pltpu
from jax.sharding import PartitionSpec as P

MESH = pl.DeviceIdType.MESH
RIGHT, LEFT = 0, 1


def compact(expert_ids, tokens, grads, capacity):
    slot_order = jnp.arange(capacity, dtype=jnp.int32)[:, None]
    choosers = []
    for expert in range(grads.shape[0]):
        routed = jnp.any(expert_ids == expert, axis=1)
        slot_index = jnp.cumsum(routed.astype(jnp.int32)) - 1
        chosen = jnp.logical_and(routed[None, :], slot_index[None, :] == slot_order)
        choosers.append(chosen.astype(jnp.bfloat16))
    chooser = jnp.stack(choosers)
    picked_act = jnp.einsum(
        "ect,td->ecd", chooser, tokens, preferred_element_type=jnp.float32
    ).astype(jnp.bfloat16)
    picked_grad = jnp.einsum(
        "ect,etf->ecf", chooser, grads, preferred_element_type=jnp.float32
    ).astype(jnp.bfloat16)
    return (picked_act, picked_grad)


def ring_place(index, size):
    return jnp.where(lax.rem(index, 2) == 0, index // 2, size - 1 - index // 2)


def ring_index(place, size):
    place = lax.rem(place + 2 * size, size)
    return jnp.where(place < size // 2, 2 * place, 2 * (size - 1 - place) + 1)


def exchange_kernel(
    n, m, share, picked_act, picked_grad, act_basis, grad_basis, act_sq, grad_sq,
    act_w, grad_w, rows_in, part, sums, grad_all, grad_part, grad_in,
    load_sem, tok_send, tok_recv, share_send, share_recv, sum_send, sum_recv,
    grad_send, grad_recv, act_send, act_recv, part_send, part_recv, sq_send, sq_recv,
):
    half = n // 2
    experts, cap, _ = picked_grad.shape
    feats = act_basis.shape[1]
    columns = grad_basis.shape[2]
    act_columns = act_basis.shape[2]
    me = lax.axis_index("dp")
    mine = lax.axis_index("owner")
    place = ring_place(me, n)
    towards = (ring_index(place + 1, n), ring_index(place - 1, n))

    def rows(index):
        return pl.ds(pl.multiple_of(index * cap, cap), cap)

    def remote(src, dst, send, recv, **device):
        return pltpu.make_async_remote_copy(
            src_ref=src, dst_ref=dst, send_sem=send, recv_sem=recv,
            device_id=device, device_id_type=MESH,
        )

    load_act = pltpu.make_async_copy(act_basis, act_w, load_sem.at[0])
    load_grad = pltpu.make_async_copy(grad_basis, grad_w, load_sem.at[1])
    load_grad.start()
    load_act.start()

    barrier = pltpu.get_barrier_semaphore()

    @pl.loop(1, n)
    def _(k):
        pl.semaphore_signal(barrier, inc=1, device_id={"dp": lax.rem(me + k, n)}, device_id_type=MESH)

    @pl.loop(1, m)
    def _(k):
        pl.semaphore_signal(barrier, inc=1, device_id={"owner": lax.rem(mine + k, m)}, device_id_type=MESH)

    pl.semaphore_wait(barrier, n + m - 2)

    share_rows = experts * cap // share
    my_share = lax.rem(mine, share)
    share_base = mine - my_share
    my_rows = pl.ds(pl.multiple_of(my_share * share_rows, share_rows), share_rows)

    def features(index):
        return pl.ds(pl.multiple_of(index * feats, feats), feats)

    def token_copy(k):
        to = lax.rem(me + k, n)
        return remote(
            picked_act.at[my_rows, features(to)], rows_in.at[me, my_rows, :],
            tok_send.at[k], tok_recv.at[k], dp=to,
        )

    @pl.loop(1, n)
    def _(k):
        token_copy(k).start()

    own_rows = pltpu.make_async_copy(
        picked_act.at[my_rows, features(me)], rows_in.at[me, my_rows, :], load_sem.at[2]
    )
    own_rows.start()

    def gather_has(way, step, e):
        return step < half - 1 or (step == half - 1 and e % 2 == way)

    def gather_copy(buf, own, send, recv, way, step, e):
        chunk = rows(ring_index(place - step if way == RIGHT else place + step, n))
        src = own.at[e] if own is not None and step == 0 else buf.at[e, chunk, :]
        return remote(
            src, buf.at[e, chunk, :], send.at[way, step, e], recv.at[way, step, e], dp=towards[way]
        )

    def gather_step(buf, own, send, recv, step):
        for e in range(experts):
            for way in (RIGHT, LEFT):
                if step > 0 and gather_has(way, step - 1, e):
                    gather_copy(buf, own, send, recv, way, step - 1, e).wait_recv()
                if gather_has(way, step, e):
                    gather_copy(buf, own, send, recv, way, step, e).start()

    def gather_end(buf, own, send, recv):
        for step in range(half):
            for e in range(experts):
                for way in (RIGHT, LEFT):
                    if gather_has(way, step, e):
                        gather_copy(buf, own, send, recv, way, step, e).wait_send()

    grad_ring = (grad_all, picked_grad, grad_send, grad_recv)
    act_ring = (act_sq, None, act_send, act_recv)
    gather_step(*grad_ring, 0)

    units = {}
    for step in range(half + 1):
        units[step] = []
        for e in range(experts):
            for way in (RIGHT, LEFT) if 0 < step < half else (RIGHT,):
                units[step].append((way, e))
    first = {step: sum(len(units[s]) for s in range(step)) for step in units}

    def unit_rows(step, way):
        return rows(ring_index(place - step if way == RIGHT else place + step, n))

    tile = min(256, columns)

    def project(step):
        for e in range(experts):
            ways = [w for (w, x) in units[step] if x == e]
            at = [first[step] + units[step].index((w, e)) for w in ways]

            @pl.loop(0, columns // tile)
            def _(c):
                cols = pl.ds(pl.multiple_of(c * tile, tile), tile)
                if step == 0:
                    lhs = picked_grad[e]
                else:
                    lhs = jnp.concatenate([grad_all[e, unit_rows(step, w), :] for w in ways], axis=0)
                out = jnp.dot(lhs, grad_w[e, :, cols], preferred_element_type=jnp.float32)
                for i, u in enumerate(at):
                    grad_part[u, :, cols] = out[i * cap : (i + 1) * cap]

        for i in range(len(units[step])):
            u = first[step] + i

            @pl.when(mine != u % m)
            def _():
                part_copy(u).start()

    def part_copy(u):
        q, k = u % m, u // m
        slot = lax.rem(mine - q - 1 + 2 * m, m)
        return remote(
            grad_part.at[u], grad_in.at[k, slot], part_send.at[u], part_recv.at[k, slot], owner=q
        )

    def square_copy(u, step, way, e, j):
        chunk = unit_rows(step, way)
        return remote(
            grad_sq.at[e, chunk, :], grad_sq.at[e, chunk, :],
            sq_send.at[u // m, j - 1], sq_recv.at[u], owner=lax.rem(mine + j, m),
        )

    def reduce(step):
        for i, (way, e) in enumerate(units[step]):
            u = first[step] + i
            q, k = u % m, u // m

            @pl.when(mine == q)
            def _():
                total = grad_part[u]
                for slot in range(m - 1):
                    pltpu.make_async_copy(
                        grad_in.at[k, slot], grad_in.at[k, slot], part_recv.at[k, slot]
                    ).wait()
                    total = total + grad_in[k, slot]
                grad_sq[e, unit_rows(step, way), :] = jnp.square(total).astype(jnp.bfloat16)
                for j in range(1, m):
                    square_copy(u, step, way, e, j).start()

    def sum_has(way, step, e):
        return 0 < step < half or (step == 0 and e % 2 == way)

    def sum_rows(way, step):
        return rows(ring_index(place + (half - step) if way == RIGHT else place - (half - step), n))

    def sum_copy(way, step, e):
        return remote(
            part.at[e, sum_rows(way, step), :], sums.at[way, step, e],
            sum_send.at[way, step, e], sum_recv.at[way, step, e], dp=towards[way],
        )

    def sum_step(step):
        for e in range(experts):
            for way in (RIGHT, LEFT):
                if step > 0 and sum_has(way, step - 1, e):
                    sum_copy(way, step - 1, e).wait_recv()
                    there = sum_rows(way, step)
                    part[e, there, :] = part[e, there, :] + sums[way, step - 1, e]
                if sum_has(way, step, e):
                    sum_copy(way, step, e).start()

    load_grad.wait()
    project(0)

    @pl.loop(1, n)
    def _(k):
        token_copy(k).wait_recv()

    own_rows.wait()

    def share_copy(k):
        return remote(
            rows_in.at[:, my_rows, :], rows_in.at[:, my_rows, :],
            share_send.at[k], share_recv.at[k], owner=share_base + lax.rem(my_share + k, share),
        )

    for k in range(1, share):
        share_copy(k).start()
    if half > 1:
        gather_step(*grad_ring, 1)
    reduce(0)
    for k in range(1, share):
        share_copy(k).wait_recv()
    load_act.wait()
    act_tile = min(256, act_columns)
    for e in range(experts):

        @pl.loop(0, act_columns // act_tile)
        def _(c):
            cols = pl.ds(pl.multiple_of(c * act_tile, act_tile), act_tile)
            lhs = rows_in[:, e * cap : (e + 1) * cap, :].reshape(n * cap, feats)
            part[e, :, cols] = jnp.dot(lhs, act_w[e, :, cols], preferred_element_type=jnp.float32)

    sum_step(0)
    for step in range(1, half):
        project(step)
        sum_step(step)
        gather_step(*grad_ring, step + 1)
        reduce(step)

    for e in range(experts):
        total = part[e, rows(me), :]
        for way in (RIGHT, LEFT):
            if sum_has(way, half - 1, e):
                sum_copy(way, half - 1, e).wait_recv()
                total = total + sums[way, half - 1, e]
        rounded = total.astype(jnp.bfloat16).astype(jnp.float32)
        act_sq[e, rows(me), :] = jnp.square(rounded).astype(jnp.bfloat16)
        for way in (RIGHT, LEFT):
            if gather_has(way, 0, e):
                gather_copy(*act_ring, way, 0, e).start()
    if half == 1:
        gather_step(*grad_ring, 1)
    project(half)
    for step in range(1, half + 1):
        gather_step(*act_ring, step)
        if step == 1:
            reduce(half)

    for step in units:
        for i, (way, e) in enumerate(units[step]):
            u = first[step] + i

            @pl.when(mine == u % m)
            def _():
                for j in range(1, m):
                    square_copy(u, step, way, e, j).wait_send()

            @pl.when(mine != u % m)
            def _():
                part_copy(u).wait_send()
                square_copy(u, step, way, e, 1).wait_recv()

    @pl.loop(1, n)
    def _(k):
        token_copy(k).wait_send()

    for k in range(1, share):
        share_copy(k).wait_send()
    for step in range(half):
        for e in range(experts):
            for way in (RIGHT, LEFT):
                if sum_has(way, step, e):
                    sum_copy(way, step, e).wait_send()
    gather_end(*grad_ring)
    gather_end(*act_ring)


def exchange(picked_act, picked_grad, act_basis, grad_basis):
    n, m = lax.axis_size("dp"), lax.axis_size("owner")
    experts, cap, window = picked_grad.shape
    feats, act_columns = act_basis.shape[1:]
    columns = grad_basis.shape[2]
    half, count = n // 2, n * experts
    share = min(m, experts * cap // 16)
    kept = -(-count // m)
    dma = pltpu.SemaphoreType.DMA
    vmem = pl.BlockSpec(memory_space=pltpu.VMEM)
    flops = 2 * n * cap * experts * (feats * act_columns + window * columns)
    return pl.pallas_call(
        functools.partial(exchange_kernel, n, m, share),
        out_shape=(
            jax.ShapeDtypeStruct((experts, n * cap, act_columns), jnp.bfloat16),
            jax.ShapeDtypeStruct((experts, n * cap, columns), jnp.bfloat16),
        ),
        in_specs=[vmem, vmem, pl.BlockSpec(memory_space=pl.ANY), pl.BlockSpec(memory_space=pl.ANY)],
        out_specs=(vmem, vmem),
        scratch_shapes=[
            pltpu.VMEM(act_basis.shape, jnp.bfloat16),
            pltpu.VMEM(grad_basis.shape, jnp.bfloat16),
            pltpu.VMEM((n, experts * cap, feats), jnp.bfloat16),
            pltpu.VMEM((experts, n * cap, act_columns), jnp.float32),
            pltpu.VMEM((2, half, experts, cap, act_columns), jnp.float32),
            pltpu.VMEM((experts, n * cap, window), jnp.bfloat16),
            pltpu.VMEM((count, cap, columns), jnp.float32),
            pltpu.VMEM((kept, m - 1, cap, columns), jnp.float32),
            dma((3,)),
            dma((n,)),
            dma((n,)),
            dma((share,)),
            dma((share,)),
            dma((2, half, experts)),
            dma((2, half, experts)),
            dma((2, half, experts)),
            dma((2, half, experts)),
            dma((2, half, experts)),
            dma((2, half, experts)),
            dma((count,)),
            dma((kept, m - 1)),
            dma((kept, m - 1)),
            dma((count,)),
        ],
        compiler_params=pltpu.CompilerParams(
            collective_id=0, has_side_effects=True, vmem_limit_bytes=58 * 2**20
        ),
        cost_estimate=pl.CostEstimate(flops=flops, bytes_accessed=20 * 2**20, transcendentals=0),
    )(picked_act.reshape(experts * cap, picked_act.shape[2]), picked_grad, act_basis, grad_basis)


def per_device(tokens, act_basis, grad_basis, grads, expert_ids):
    tok_rows = tokens.shape[0]
    token_total = tok_rows * lax.axis_size("dp")
    picked_act, picked_grad = compact(expert_ids, tokens, grads, tok_rows // 2)
    act_sq, grad_sq = exchange(picked_act, picked_grad, act_basis, grad_basis)
    return (
        jnp.einsum("erk,era->eka", grad_sq, act_sq, preferred_element_type=jnp.float32)
        / token_total
    )


def solution(mesh):
    placed = (
        P("dp", None),
        P(None, "dp", "owner"),
        P(None, "owner", "dp"),
        P(None, "dp", "owner"),
        P("dp", None),
    )
    return jax.shard_map(
        per_device, mesh=mesh, in_specs=placed, out_specs=P(None, "dp", "owner"), check_vma=False
    )
```

time: 330 us -> 132 us (0.40)
  waiting for transfers between devices: 224 us -> 0 us
  Pallas kernels: 0 us -> 119 us
  blocking collectives: 41.6 us -> 0 us
  local copies, waits for them, and re-layouts: 16.4 us -> 0.23 us
  matrix products: 26.4 us -> 11.7 us
  between operations: 13.2 us -> 0.04 us
  other arithmetic: 5.3 us -> 1.37 us
    reduce_scatter x2 -> x0, waiting for transfers between devices: 126 us -> none  [the longest x1 81.4 us: per_device(): lax.psum_scatter(act_part, 'dp', scatter_dimension=1, tiled=True)]
    pallas_call x0 -> x1, Pallas kernels: none -> 119 us  [exchange(): pl.pallas_call(functools.partial(exchange_kernel, n, m, share), out_shape...]
    all_gather x3 -> x0, waiting for transfers between devices: 98.6 us -> none  [the longest x1 48.3 us: per_device(): act_all = lax.all_gather(act_own, 'dp', axis=1, tiled=True)]
    all_to_all x1 -> x0, blocking collectives: 41.6 us -> none  [per_device(): lax.all_to_all(picked_act, 'dp', split_axis=2, concat_axis=1, tiled=True)]
    dot_general x2 -> x0, matrix products: 14.4 us -> none  [the longest x1 11.2 us: per_device(): jnp.einsum('erf,efk->erk', grad_rows, grad_basis, preferred_element_type=...]
    unnamed x4 -> x2, local copies, waits for them, and re-layouts: 7.71 us -> 0.01 us
    all_to_all x1 -> x0, local copies, waits for them, and re-layouts: 4.62 us -> none  [per_device(): lax.all_to_all(picked_act, 'dp', split_axis=2, concat_axis=1, tiled=True)]
    convert_element_type x1 -> x0, local copies, waits for them, and re-layouts: 3.89 us -> none  [compact(): picked_act = jnp.einsum('ect,td->ecd', chooser, tokens, preferred_element...]
  transfers between devices with their start and end apart: 5 -> 0, of which waited for: 5 -> 0; matrix products, arithmetic and copies ran while one was open for 11% -> 0% of each run, Pallas kernels for 0% -> 0%
where the time goes in v2:
time: 132 us
  Pallas kernels  119 us (90%)
  matrix products  11.7 us (9%)
  other arithmetic  1.37 us (1%)
    pallas_call x1, Pallas kernels, exchange(): pl.pallas_call(functools.partial(exchange_kernel, n, m, share), out_shape...  119 us
    dot_general x1, matrix products, per_device(): jnp.einsum('erk,era->eka', grad_sq, act_sq, preferred_element_type=jnp.fl...  8 us

profile of v2, /device:TPU:15, one launch (start us, length us, event | category | flops | bytes accessed | tf_op | source)
XLA Modules:
  0.0 132.0 jit_solution(5616171068852473575)
XLA Ops:
  0.0 0.0 copy-start
  0.0 0.8 compare_reduce_fusion.1
  0.8 0.1 copy.10
  0.9 0.2 reduce-window.17
  1.1 0.1 add_reduce_fusion
  1.2 0.1 copy.9
  1.3 0.2 reduce-window.16
  1.5 0.1 add_reduce_fusion.1
  1.6 2.3 %convolution_convert_fusion.1.picked_grad = bf16[2,64,2048]{2,1,0:T(8,128)(2,1)} fusion(bf16[2,128,2048]{2,1,0:T(8,128)(2,1)} %param.8, pred[1,64,128]{2,1,0:T(32,128)(4,1)S(1)} %get-tuple-element.12, pred[1,64,128]{2,1,0:T(32,128)(4,1)S(1)} %get-tuple-element.11), kind=kOutput, calls=%fused_computation.2 | convolution fusion | flops 67387392 | bytes 1589248 | tf_op jit(solution)/shard_map/ect,etf->ecf/dot_general | solution.py:26
  3.9 0.0 copy-done
  3.9 1.4 %convolution_convert_fusion = bf16[2,64,4096]{2,1,0:T(8,128)(2,1)} fusion(bf16[128,4096]{1,0:T(8,128)(2,1)S(1)} %copy-done, pred[1,64,128]{2,1,0:T(32,128)(4,1)S(1)} %get-tuple-element.12, pred[1,64,128]{2,1,0:T(32,128)(4,1)S(1)} %get-tuple-element.11), kind=kOutput, calls=%fused_computation | convolution fusion | flops 134758400 | bytes 2113536 | tf_op jit(solution)/shard_map/ect,td->ecd/dot_general | solution.py:23
  5.3 118.7 %shard_map.55 = (bf16[2,512,1024]{2,1,0:T(8,128)(2,1)}, bf16[2,512,1024]{2,1,0:T(8,128)(2,1)}) custom-call(bf16[128,4096]{1,0:T(8,128)(2,1)} %bitcast.11, bf16[2,64,2048]{2,1,0:T(8,128)(2,1)} %convolution_convert_fusion.1.picked_grad, bf16[2,512,1024]{2,1,0:T(8,128)(2,1)} %act_basis.1, bf16[2,2048,1024]{2,1,0:T(8,128)(2,1)} %grad_basis.1), custom_call_target="tpu_custom_call" | custom-call | flops 5368709120 | bytes 20971520 | tf_op jit(solution)/shard_map/pallas_call | solution.py:323
  124.0 8.0 %broadcast_multiply_fusion = f32[2,1024,1024]{2,1,0:T(8,128)} fusion(bf16[2,512,1024]{2,1,0:T(8,128)(2,1)} %get-tuple-element.7, bf16[2,512,1024]{2,1,0:T(8,128)(2,1)} %get-tuple-element.8), kind=kOutput, calls=%fused_computation.1 | convolution fusion | flops 2149580800 | bytes 12582912 | tf_op jit(solution)/shard_map/erk,era->eka/dot_general | solution.py:369
  (3 shorter events, 0.0 us)
Async XLA Ops:
  0.0 3.9 %copy-start = (bf16[128,4096]{1,0:T(8,128)(2,1)S(1)}, bf16[128,4096]{1,0:T(8,128)(2,1)}, u32[]{:S(2)}) copy-start(bf16[128,4096]{1,0:T(8,128)(2,1)} %param.5) | copy-start | bytes 3145732

commit v3 on v2

--- a/solution.py
+++ b/solution.py
@@ -11,22 +11,15 @@
 RIGHT, LEFT = 0, 1
 
 
-def compact(expert_ids, tokens, grads, capacity):
+def choose(expert_ids, experts, capacity):
     slot_order = jnp.arange(capacity, dtype=jnp.int32)[:, None]
     choosers = []
-    for expert in range(grads.shape[0]):
+    for expert in range(experts):
         routed = jnp.any(expert_ids == expert, axis=1)
         slot_index = jnp.cumsum(routed.astype(jnp.int32)) - 1
         chosen = jnp.logical_and(routed[None, :], slot_index[None, :] == slot_order)
         choosers.append(chosen.astype(jnp.bfloat16))
-    chooser = jnp.stack(choosers)
-    picked_act = jnp.einsum(
-        "ect,td->ecd", chooser, tokens, preferred_element_type=jnp.float32
-    ).astype(jnp.bfloat16)
-    picked_grad = jnp.einsum(
-        "ect,etf->ecf", chooser, grads, preferred_element_type=jnp.float32
-    ).astype(jnp.bfloat16)
-    return (picked_act, picked_grad)
+    return jnp.stack(choosers)
 
 
 def ring_place(index, size):
@@ -39,8 +32,8 @@
 
 
 def exchange_kernel(
-    n, m, share, picked_act, picked_grad, act_basis, grad_basis, act_sq, grad_sq,
-    act_w, grad_w, rows_in, part, sums, grad_all, grad_part, grad_in,
+    n, m, share, chooser, tokens, grads, act_basis, grad_basis, act_sq, grad_sq,
+    picked_act, picked_grad, first_out, first_in, act_w, grad_w, rows_in, part, sums, grad_all, grad_part, grad_in,
     load_sem, tok_send, tok_recv, share_send, share_recv, sum_send, sum_recv,
     grad_send, grad_recv, act_send, act_recv, part_send, part_recv, sq_send, sq_recv,
 ):
@@ -78,6 +71,20 @@
     def _(k):
         pl.semaphore_signal(barrier, inc=1, device_id={"owner": lax.rem(mine + k, m)}, device_id_type=MESH)
 
+    for e in range(experts):
+        for width, source, target in (
+            (tokens.shape[1], tokens, picked_act.at[e * cap : (e + 1) * cap]),
+            (grads.shape[2], grads.at[e], picked_grad.at[e]),
+        ):
+            pick_tile = min(512, width)
+
+            @pl.loop(0, width // pick_tile)
+            def _(c):
+                cols = pl.ds(pl.multiple_of(c * pick_tile, pick_tile), pick_tile)
+                target[:, cols] = jnp.dot(
+                    chooser[e], source[:, cols], preferred_element_type=jnp.float32
+                ).astype(jnp.bfloat16)
+
     pl.semaphore_wait(barrier, n + m - 2)
 
     share_rows = experts * cap // share
@@ -206,11 +213,21 @@
     def sum_rows(way, step):
         return rows(ring_index(place + (half - step) if way == RIGHT else place - (half - step), n))
 
+    def sum_first(way, step, e):
+        return step == 0 or (step == 1 and e % 2 != way)
+
     def sum_copy(way, step, e):
-        return remote(
-            part.at[e, sum_rows(way, step), :], sums.at[way, step, e],
+        narrow = sum_first(way, step, e)
+        return remote(
+            first_out.at[way, e] if narrow else part.at[e, sum_rows(way, step), :],
+            first_in.at[way, e] if narrow else sums.at[way, step, e],
             sum_send.at[way, step, e], sum_recv.at[way, step, e], dp=towards[way],
         )
+
+    def sum_arrived(way, step, e):
+        if sum_first(way, step, e):
+            return first_in[way, e].astype(jnp.float32)
+        return sums[way, step, e]
 
     def sum_step(step):
         for e in range(experts):
@@ -218,8 +235,10 @@
                 if step > 0 and sum_has(way, step - 1, e):
                     sum_copy(way, step - 1, e).wait_recv()
                     there = sum_rows(way, step)
-                    part[e, there, :] = part[e, there, :] + sums[way, step - 1, e]
+                    part[e, there, :] = part[e, there, :] + sum_arrived(way, step - 1, e)
                 if sum_has(way, step, e):
+                    if sum_first(way, step, e):
+                        first_out[way, e] = part[e, sum_rows(way, step), :].astype(jnp.bfloat16)
                     sum_copy(way, step, e).start()
 
     load_grad.wait()
@@ -266,7 +285,7 @@
         for way in (RIGHT, LEFT):
             if sum_has(way, half - 1, e):
                 sum_copy(way, half - 1, e).wait_recv()
-                total = total + sums[way, half - 1, e]
+                total = total + sum_arrived(way, half - 1, e)
         rounded = total.astype(jnp.bfloat16).astype(jnp.float32)
         act_sq[e, rows(me), :] = jnp.square(rounded).astype(jnp.bfloat16)
         for way in (RIGHT, LEFT):
@@ -309,9 +328,10 @@
     gather_end(*act_ring)
 
 
-def exchange(picked_act, picked_grad, act_basis, grad_basis):
+def exchange(chooser, tokens, grads, act_basis, grad_basis):
     n, m = lax.axis_size("dp"), lax.axis_size("owner")
-    experts, cap, window = picked_grad.shape
+    experts, cap, _ = chooser.shape
+    window = grads.shape[2]
     feats, act_columns = act_basis.shape[1:]
     columns = grad_basis.shape[2]
     half, count = n // 2, n * experts
@@ -326,9 +346,13 @@
             jax.ShapeDtypeStruct((experts, n * cap, act_columns), jnp.bfloat16),
             jax.ShapeDtypeStruct((experts, n * cap, columns), jnp.bfloat16),
         ),
-        in_specs=[vmem, vmem, pl.BlockSpec(memory_space=pl.ANY), pl.BlockSpec(memory_space=pl.ANY)],
+        in_specs=[vmem, vmem, vmem, pl.BlockSpec(memory_space=pl.ANY), pl.BlockSpec(memory_space=pl.ANY)],
         out_specs=(vmem, vmem),
         scratch_shapes=[
+            pltpu.VMEM((experts * cap, tokens.shape[1]), jnp.bfloat16),
+            pltpu.VMEM((experts, cap, window), jnp.bfloat16),
+            pltpu.VMEM((2, experts, cap, act_columns), jnp.bfloat16),
+            pltpu.VMEM((2, experts, cap, act_columns), jnp.bfloat16),
             pltpu.VMEM(act_basis.shape, jnp.bfloat16),
             pltpu.VMEM(grad_basis.shape, jnp.bfloat16),
             pltpu.VMEM((n, experts * cap, feats), jnp.bfloat16),
@@ -357,18 +381,41 @@
             collective_id=0, has_side_effects=True, vmem_limit_bytes=58 * 2**20
         ),
         cost_estimate=pl.CostEstimate(flops=flops, bytes_accessed=20 * 2**20, transcendentals=0),
-    )(picked_act.reshape(experts * cap, picked_act.shape[2]), picked_grad, act_basis, grad_basis)
+    )(chooser, tokens, grads, act_basis, grad_basis)
+
+
+def moment_kernel(token_total, grad_sq, act_sq, out):
+    out[0] = (
+        lax.dot_general(
+            grad_sq[0], act_sq[0], (((0,), (0,)), ((), ())), preferred_element_type=jnp.float32
+        )
+        / token_total
+    )
+
+
+def moment(grad_sq, act_sq, token_total):
+    experts, slots, columns = grad_sq.shape
+    act_columns = act_sq.shape[2]
+    tile = min(256, columns)
+    return pl.pallas_call(
+        functools.partial(moment_kernel, token_total),
+        out_shape=jax.ShapeDtypeStruct((experts, columns, act_columns), jnp.float32),
+        grid=(experts, columns // tile),
+        in_specs=[
+            pl.BlockSpec((1, slots, tile), lambda e, k: (e, 0, k)),
+            pl.BlockSpec((1, slots, act_columns), lambda e, k: (e, 0, 0)),
+        ],
+        out_specs=pl.BlockSpec((1, tile, act_columns), lambda e, k: (e, k, 0)),
+        compiler_params=pltpu.CompilerParams(vmem_limit_bytes=32 * 2**20),
+    )(grad_sq, act_sq)
 
 
 def per_device(tokens, act_basis, grad_basis, grads, expert_ids):
     tok_rows = tokens.shape[0]
     token_total = tok_rows * lax.axis_size("dp")
-    picked_act, picked_grad = compact(expert_ids, tokens, grads, tok_rows // 2)
-    act_sq, grad_sq = exchange(picked_act, picked_grad, act_basis, grad_basis)
-    return (
-        jnp.einsum("erk,era->eka", grad_sq, act_sq, preferred_element_type=jnp.float32)
-        / token_total
-    )
+    chooser = choose(expert_ids, grads.shape[0], tok_rows // 2)
+    act_sq, grad_sq = exchange(chooser, tokens, grads, act_basis, grad_basis)
+    return moment(grad_sq, act_sq, token_total)
 
 
 def solution(mesh):

time: 132 us -> 128 us (0.970); the launches traced: 132 us -> 127 us
  matrix products: 11.7 us -> 0 us
  local copies, waits for them, and re-layouts: 0.23 us -> 3.4 us
  Pallas kernels: 119 us -> 121 us
    dot_general x3 -> x0, matrix products: 11.7 us -> none  [the longest x1 8 us: per_device(): jnp.einsum('erk,era->eka', grad_sq, act_sq, preferred_element_type=jnp.fl...]
    pallas_call x0 -> x1, Pallas kernels: none -> 6.39 us  [moment(): pl.pallas_call(functools.partial(moment_kernel, token_total), out_shape=j...]
    pallas_call x1, Pallas kernels: 119 us -> 115 us  [exchange(): pl.pallas_call(functools.partial(exchange_kernel, n, m, share), out_shape...]
    unnamed x2 -> x4, local copies, waits for them, and re-layouts: 0.01 us -> 3.17 us
where the time goes in v3:
time: 128 us; the launch traced here: 127 us
  Pallas kernels  121 us (95%)
  local copies, waits for them, and re-layouts  3.4 us (3%)
  other arithmetic  1.91 us (1%)
    pallas_call x1, Pallas kernels, exchange(): pl.pallas_call(functools.partial(exchange_kernel, n, m, share), out_shape...  115 us
    pallas_call x1, Pallas kernels, moment(): pl.pallas_call(functools.partial(moment_kernel, token_total), out_shape=j...  6.39 us
    unnamed x4, local copies, waits for them, and re-layouts  3.17 us

profile of v3, /device:TPU:15, one launch (start us, length us, event | category | flops | bytes accessed | tf_op | source)
XLA Modules:
  0.0 126.6 jit_solution(17200684760130722542)
XLA Ops:
  0.0 0.7 compare_reduce_fusion.1
  0.7 0.1 copy.9
  0.8 0.2 reduce-window.17
  1.0 0.1 add_reduce_fusion
  1.1 0.1 copy.8
  1.2 0.2 reduce-window.16
  1.4 0.1 add_reduce_fusion.1
  1.5 0.6 add_convert_fusion.chooser
  2.2 114.9 %shard_map.55 = (bf16[2,512,1024]{2,1,0:T(8,128)(2,1)}, bf16[2,512,1024]{2,1,0:T(8,128)(2,1)}) custom-call(bf16[2,64,128]{2,1,0:T(8,128)(2,1)} %add_convert_fusion.chooser, bf16[128,4096]{1,0:T(8,128)(2,1)} %tokens.1, bf16[2,128,2048]{2,1,0:T(8,128)(2,1)} %grads.1, bf16[2,512,1024]{2,1,0:T(8,128)(2,1)} %act_basis.1, bf16[2,2048,1024]{2,1,0:T(8,128)(2,1)} %grad_basis.1), custom_call_target="tpu_custom_call" | custom-call | flops 5368709120 | bytes 20971520 | tf_op jit(solution)/shard_map/pallas_call | solution.py:343
  117.1 0.0 copy-start
  117.1 1.6 %copy-done = bf16[2,512,1024]{2,1,0:T(8,128)(2,1)S(1)} copy-done((bf16[2,512,1024]{2,1,0:T(8,128)(2,1)S(1)}, bf16[2,512,1024]{2,1,0:T(8,128)(2,1)}, u32[]{:S(2)}) %copy-start) | copy-done | bytes 2097176
  118.7 0.0 copy-start.1
  118.7 1.6 %copy-done.1 = bf16[2,512,1024]{2,1,0:T(8,128)(2,1)S(1)} copy-done((bf16[2,512,1024]{2,1,0:T(8,128)(2,1)S(1)}, bf16[2,512,1024]{2,1,0:T(8,128)(2,1)}, u32[]{:S(2)}) %copy-start.1) | copy-done | bytes 2097176
  120.2 6.4 %shard_map.56 = f32[2,1024,1024]{2,1,0:T(8,128)} custom-call(bf16[2,512,1024]{2,1,0:T(8,128)(2,1)S(1)} %copy-done.1, bf16[2,512,1024]{2,1,0:T(8,128)(2,1)S(1)} %copy-done), custom_call_target="tpu_custom_call" | custom-call | tf_op jit(solution)/shard_map/pallas_call | solution.py:400
  (3 shorter events, 0.0 us)
Async XLA Ops:
  117.1 1.6 %copy-start = (bf16[2,512,1024]{2,1,0:T(8,128)(2,1)S(1)}, bf16[2,512,1024]{2,1,0:T(8,128)(2,1)}, u32[]{:S(2)}) copy-start(bf16[2,512,1024]{2,1,0:T(8,128)(2,1)} %get-tuple-element.8.act_sq) | copy-start | bytes 6291460
  118.7 1.6 %copy-start.1 = (bf16[2,512,1024]{2,1,0:T(8,128)(2,1)S(1)}, bf16[2,512,1024]{2,1,0:T(8,128)(2,1)}, u32[]{:S(2)}) copy-start(bf16[2,512,1024]{2,1,0:T(8,128)(2,1)} %get-tuple-element.7.grad_sq) | copy-start | bytes 6291460

commit v4 on v3

--- a/solution.py
+++ b/solution.py
@@ -9,6 +9,28 @@
 
 MESH = pl.DeviceIdType.MESH
 RIGHT, LEFT = 0, 1
+KNEE, TOP = 8.0, 32767.0
+
+
+def encode(value):
+    code = TOP * value / (jnp.abs(value) + KNEE)
+    return (code + jnp.where(value >= 0, 0.5, -0.5)).astype(jnp.int32).astype(jnp.int16)
+
+
+def decode(code):
+    code = code.astype(jnp.int32).astype(jnp.float32)
+    return KNEE * code / (TOP - jnp.abs(code))
+
+
+def power_scale(norm_sq):
+    scale, inverse = jnp.full_like(norm_sq, 0.25), jnp.full_like(norm_sq, 4.0)
+    norm_sq = norm_sq * 0.0625
+    for k in (16, 8, 4, 2, 1):
+        more = norm_sq * 4.0**k < 16384.0
+        scale = jnp.where(more, scale * 2.0**k, scale)
+        inverse = jnp.where(more, inverse * 0.5**k, inverse)
+        norm_sq = jnp.where(more, norm_sq * 4.0**k, norm_sq)
+    return scale, inverse
 
 
 def choose(expert_ids, experts, capacity):
@@ -33,7 +55,7 @@
 
 def exchange_kernel(
     n, m, share, chooser, tokens, grads, act_basis, grad_basis, act_sq, grad_sq,
-    picked_act, picked_grad, first_out, first_in, act_w, grad_w, rows_in, part, sums, grad_all, grad_part, grad_in,
+    picked_act, picked_grad, unscale, sum_out, sum_in, act_w, grad_w, rows_in, part, grad_all, grad_part, grad_in,
     load_sem, tok_send, tok_recv, share_send, share_recv, sum_send, sum_recv,
     grad_send, grad_recv, act_send, act_recv, part_send, part_recv, sq_send, sq_recv,
 ):
@@ -85,6 +107,11 @@
                     chooser[e], source[:, cols], preferred_element_type=jnp.float32
                 ).astype(jnp.bfloat16)
 
+        row = picked_act[e * cap : (e + 1) * cap].astype(jnp.float32)
+        scale, inverse = power_scale(jnp.sum(row * row, axis=1, keepdims=True))
+        picked_act[e * cap : (e + 1) * cap] = (row * scale).astype(jnp.bfloat16)
+        unscale[e] = jnp.broadcast_to(inverse, unscale.shape[1:])
+
     pl.semaphore_wait(barrier, n + m - 2)
 
     share_rows = experts * cap // share
@@ -213,33 +240,23 @@
     def sum_rows(way, step):
         return rows(ring_index(place + (half - step) if way == RIGHT else place - (half - step), n))
 
-    def sum_first(way, step, e):
-        return step == 0 or (step == 1 and e % 2 != way)
-
     def sum_copy(way, step, e):
-        narrow = sum_first(way, step, e)
-        return remote(
-            first_out.at[way, e] if narrow else part.at[e, sum_rows(way, step), :],
-            first_in.at[way, e] if narrow else sums.at[way, step, e],
+        return remote(
+            sum_out.at[way, step, e], sum_in.at[way, step, e],
             sum_send.at[way, step, e], sum_recv.at[way, step, e], dp=towards[way],
         )
-
-    def sum_arrived(way, step, e):
-        if sum_first(way, step, e):
-            return first_in[way, e].astype(jnp.float32)
-        return sums[way, step, e]
 
     def sum_step(step):
         for e in range(experts):
             for way in (RIGHT, LEFT):
+                if not sum_has(way, step, e):
+                    continue
+                total = part[e, sum_rows(way, step), :]
                 if step > 0 and sum_has(way, step - 1, e):
                     sum_copy(way, step - 1, e).wait_recv()
-                    there = sum_rows(way, step)
-                    part[e, there, :] = part[e, there, :] + sum_arrived(way, step - 1, e)
-                if sum_has(way, step, e):
-                    if sum_first(way, step, e):
-                        first_out[way, e] = part[e, sum_rows(way, step), :].astype(jnp.bfloat16)
-                    sum_copy(way, step, e).start()
+                    total = total + decode(sum_in[way, step - 1, e])
+                sum_out[way, step, e] = encode(total)
+                sum_copy(way, step, e).start()
 
     load_grad.wait()
     project(0)
@@ -285,8 +302,8 @@
         for way in (RIGHT, LEFT):
             if sum_has(way, half - 1, e):
                 sum_copy(way, half - 1, e).wait_recv()
-                total = total + sum_arrived(way, half - 1, e)
-        rounded = total.astype(jnp.bfloat16).astype(jnp.float32)
+                total = total + decode(sum_in[way, half - 1, e])
+        rounded = (total * unscale[e, :, :1]).astype(jnp.bfloat16).astype(jnp.float32)
         act_sq[e, rows(me), :] = jnp.square(rounded).astype(jnp.bfloat16)
         for way in (RIGHT, LEFT):
             if gather_has(way, 0, e):
@@ -351,13 +368,13 @@
         scratch_shapes=[
             pltpu.VMEM((experts * cap, tokens.shape[1]), jnp.bfloat16),
             pltpu.VMEM((experts, cap, window), jnp.bfloat16),
-            pltpu.VMEM((2, experts, cap, act_columns), jnp.bfloat16),
-            pltpu.VMEM((2, experts, cap, act_columns), jnp.bfloat16),
+            pltpu.VMEM((experts, cap, 128), jnp.float32),
+            pltpu.VMEM((2, half, experts, cap, act_columns), jnp.int16),
+            pltpu.VMEM((2, half, experts, cap, act_columns), jnp.int16),
             pltpu.VMEM(act_basis.shape, jnp.bfloat16),
             pltpu.VMEM(grad_basis.shape, jnp.bfloat16),
             pltpu.VMEM((n, experts * cap, feats), jnp.bfloat16),
             pltpu.VMEM((experts, n * cap, act_columns), jnp.float32),
-            pltpu.VMEM((2, half, experts, cap, act_columns), jnp.float32),
             pltpu.VMEM((experts, n * cap, window), jnp.bfloat16),
             pltpu.VMEM((count, cap, columns), jnp.float32),
             pltpu.VMEM((kept, m - 1, cap, columns), jnp.float32),
@@ -384,27 +401,28 @@
     )(chooser, tokens, grads, act_basis, grad_basis)
 
 
-def moment_kernel(token_total, grad_sq, act_sq, out):
+def moment_kernel(token_total, tile, grad_sq, act_sq, out):
+    e = pl.program_id(0)
+    cols = pl.ds(pl.multiple_of(pl.program_id(1) * tile, tile), tile)
     out[0] = (
         lax.dot_general(
-            grad_sq[0], act_sq[0], (((0,), (0,)), ((), ())), preferred_element_type=jnp.float32
+            grad_sq[e, :, cols], act_sq[e], (((0,), (0,)), ((), ())),
+            preferred_element_type=jnp.float32,
         )
         / token_total
     )
 
 
 def moment(grad_sq, act_sq, token_total):
-    experts, slots, columns = grad_sq.shape
+    experts, _, columns = grad_sq.shape
     act_columns = act_sq.shape[2]
     tile = min(256, columns)
+    vmem = pl.BlockSpec(memory_space=pltpu.VMEM)
     return pl.pallas_call(
-        functools.partial(moment_kernel, token_total),
+        functools.partial(moment_kernel, token_total, tile),
         out_shape=jax.ShapeDtypeStruct((experts, columns, act_columns), jnp.float32),
         grid=(experts, columns // tile),
-        in_specs=[
-            pl.BlockSpec((1, slots, tile), lambda e, k: (e, 0, k)),
-            pl.BlockSpec((1, slots, act_columns), lambda e, k: (e, 0, 0)),
-        ],
+        in_specs=[vmem, vmem],
         out_specs=pl.BlockSpec((1, tile, act_columns), lambda e, k: (e, k, 0)),
         compiler_params=pltpu.CompilerParams(vmem_limit_bytes=32 * 2**20),
     )(grad_sq, act_sq)

time: 128 us -> 125 us (0.977)
  Pallas kernels: 121 us -> 118 us
    pallas_call x1, Pallas kernels: 115 us -> 112 us  [exchange(): pl.pallas_call(functools.partial(exchange_kernel, n, m, share), out_shape...]
where the time goes in v4:
time: 125 us; the launch traced here: 123 us
  Pallas kernels  118 us (94%)
  local copies, waits for them, and re-layouts  3.4 us (3%)
  other arithmetic  1.91 us (2%)
    pallas_call x1, Pallas kernels, exchange(): pl.pallas_call(functools.partial(exchange_kernel, n, m, share), out_shape...  112 us
    pallas_call x1, Pallas kernels, moment(): pl.pallas_call(functools.partial(moment_kernel, token_total, tile), out_s...  6.26 us
    unnamed x4, local copies, waits for them, and re-layouts  3.17 us

profile of v4, /device:TPU:15, one launch (start us, length us, event | category | flops | bytes accessed | tf_op | source)
XLA Modules:
  0.0 123.4 jit_solution(5800380416531111485)
XLA Ops:
  0.0 0.7 compare_reduce_fusion.1
  0.7 0.1 copy.9
  0.8 0.2 reduce-window.17
  1.0 0.1 add_reduce_fusion
  1.1 0.1 copy.8
  1.2 0.2 reduce-window.16
  1.4 0.1 add_reduce_fusion.1
  1.5 0.6 add_convert_fusion.chooser
  2.2 111.8 %shard_map.55 = (bf16[2,512,1024]{2,1,0:T(8,128)(2,1)}, bf16[2,512,1024]{2,1,0:T(8,128)(2,1)}) custom-call(bf16[2,64,128]{2,1,0:T(8,128)(2,1)} %add_convert_fusion.chooser, bf16[128,4096]{1,0:T(8,128)(2,1)} %tokens.1, bf16[2,128,2048]{2,1,0:T(8,128)(2,1)} %grads.1, bf16[2,512,1024]{2,1,0:T(8,128)(2,1)} %act_basis.1, bf16[2,2048,1024]{2,1,0:T(8,128)(2,1)} %grad_basis.1), custom_call_target="tpu_custom_call" | custom-call | flops 5368709120 | bytes 20971520 | tf_op jit(solution)/shard_map/pallas_call | solution.py:360
  114.0 0.0 copy-start
  114.0 1.6 %copy-done = bf16[2,512,1024]{2,1,0:T(8,128)(2,1)S(1)} copy-done((bf16[2,512,1024]{2,1,0:T(8,128)(2,1)S(1)}, bf16[2,512,1024]{2,1,0:T(8,128)(2,1)}, u32[]{:S(2)}) %copy-start) | copy-done | bytes 2097176
  115.6 0.0 copy-start.1
  115.6 1.6 %copy-done.1 = bf16[2,512,1024]{2,1,0:T(8,128)(2,1)S(1)} copy-done((bf16[2,512,1024]{2,1,0:T(8,128)(2,1)S(1)}, bf16[2,512,1024]{2,1,0:T(8,128)(2,1)}, u32[]{:S(2)}) %copy-start.1) | copy-done | bytes 2097176
  117.2 6.3 %shard_map.56 = f32[2,1024,1024]{2,1,0:T(8,128)} custom-call(bf16[2,512,1024]{2,1,0:T(8,128)(2,1)S(1)} %copy-done.1, bf16[2,512,1024]{2,1,0:T(8,128)(2,1)S(1)} %copy-done), custom_call_target="tpu_custom_call" | custom-call | tf_op jit(solution)/shard_map/pallas_call | solution.py:421
  (3 shorter events, 0.0 us)
Async XLA Ops:
  114.0 1.6 %copy-start = (bf16[2,512,1024]{2,1,0:T(8,128)(2,1)S(1)}, bf16[2,512,1024]{2,1,0:T(8,128)(2,1)}, u32[]{:S(2)}) copy-start(bf16[2,512,1024]{2,1,0:T(8,128)(2,1)} %get-tuple-element.8.act_sq) | copy-start | bytes 6291460
  115.6 1.6 %copy-start.1 = (bf16[2,512,1024]{2,1,0:T(8,128)(2,1)S(1)}, bf16[2,512,1024]{2,1,0:T(8,128)(2,1)}, u32[]{:S(2)}) copy-start(bf16[2,512,1024]{2,1,0:T(8,128)(2,1)} %get-tuple-element.7.grad_sq) | copy-start | bytes 6291460

commit v5 on v4

--- a/solution.py
+++ b/solution.py
@@ -165,8 +165,6 @@
 
     grad_ring = (grad_all, picked_grad, grad_send, grad_recv)
     act_ring = (act_sq, None, act_send, act_recv)
-    gather_step(*grad_ring, 0)
-
     units = {}
     for step in range(half + 1):
         units[step] = []
@@ -258,29 +256,41 @@
                 sum_out[way, step, e] = encode(total)
                 sum_copy(way, step, e).start()
 
-    load_grad.wait()
-    project(0)
-
     @pl.loop(1, n)
     def _(k):
         token_copy(k).wait_recv()
 
     own_rows.wait()
 
+    chips = share // 2
+    core = lax.rem(my_share, 2)
+    chip = my_share // 2
+
+    def share_slice(k):
+        start = (core + 2 * lax.rem(chip - k + chips, chips)) * share_rows
+        return rows_in.at[:, pl.ds(pl.multiple_of(start, share_rows), share_rows), :]
+
     def share_copy(k):
-        return remote(
-            rows_in.at[:, my_rows, :], rows_in.at[:, my_rows, :],
-            share_send.at[k], share_recv.at[k], owner=share_base + lax.rem(my_share + k, share),
-        )
-
-    for k in range(1, share):
+        to = share_base + core + 2 * lax.rem(chip + k, chips)
+        return remote(share_slice(0), share_slice(0), share_send.at[k], share_recv.at[k], owner=to)
+
+    def pair_copy(k):
+        to = share_base + 2 * chip + 1 - core
+        at = chips + k
+        return remote(share_slice(k), share_slice(k), share_send.at[at], share_recv.at[at], owner=to)
+
+    for k in range(1, chips):
         share_copy(k).start()
-    if half > 1:
-        gather_step(*grad_ring, 1)
-    reduce(0)
-    for k in range(1, share):
+    pair_copy(0).start()
+    gather_step(*grad_ring, 0)
+    load_grad.wait()
+    project(0)
+    for k in range(1, chips):
         share_copy(k).wait_recv()
+        pair_copy(k).start()
     load_act.wait()
+    for k in range(chips):
+        pair_copy(k).wait_recv()
     act_tile = min(256, act_columns)
     for e in range(experts):
 
@@ -290,30 +300,34 @@
             lhs = rows_in[:, e * cap : (e + 1) * cap, :].reshape(n * cap, feats)
             part[e, :, cols] = jnp.dot(lhs, act_w[e, :, cols], preferred_element_type=jnp.float32)
 
+    def act_start():
+        for e in range(experts):
+            total = part[e, rows(me), :]
+            for way in (RIGHT, LEFT):
+                if sum_has(way, half - 1, e):
+                    sum_copy(way, half - 1, e).wait_recv()
+                    total = total + decode(sum_in[way, half - 1, e])
+            rounded = (total * unscale[e, :, :1]).astype(jnp.bfloat16).astype(jnp.float32)
+            act_sq[e, rows(me), :] = jnp.square(rounded).astype(jnp.bfloat16)
+            for way in (RIGHT, LEFT):
+                if gather_has(way, 0, e):
+                    gather_copy(*act_ring, way, 0, e).start()
+
     sum_step(0)
-    for step in range(1, half):
-        project(step)
-        sum_step(step)
-        gather_step(*grad_ring, step + 1)
-        reduce(step)
-
-    for e in range(experts):
-        total = part[e, rows(me), :]
-        for way in (RIGHT, LEFT):
-            if sum_has(way, half - 1, e):
-                sum_copy(way, half - 1, e).wait_recv()
-                total = total + decode(sum_in[way, half - 1, e])
-        rounded = (total * unscale[e, :, :1]).astype(jnp.bfloat16).astype(jnp.float32)
-        act_sq[e, rows(me), :] = jnp.square(rounded).astype(jnp.bfloat16)
-        for way in (RIGHT, LEFT):
-            if gather_has(way, 0, e):
-                gather_copy(*act_ring, way, 0, e).start()
-    if half == 1:
-        gather_step(*grad_ring, 1)
-    project(half)
-    for step in range(1, half + 1):
-        gather_step(*act_ring, step)
-        if step == 1:
+    done = 0
+    for hop in range(1, 2 * half + 1):
+        if hop < half:
+            sum_step(hop)
+        elif hop == half:
+            act_start()
+        else:
+            gather_step(*act_ring, hop - half)
+        while done < min(half, (2 * hop + 1) // 3):
+            done += 1
+            gather_step(*grad_ring, done)
+            project(done)
+            reduce(done - 1)
+        if hop == 2 * half - 1:
             reduce(half)
 
     for step in units:
@@ -334,8 +348,10 @@
     def _(k):
         token_copy(k).wait_send()
 
-    for k in range(1, share):
+    for k in range(1, chips):
         share_copy(k).wait_send()
+    for k in range(chips):
+        pair_copy(k).wait_send()
     for step in range(half):
         for e in range(experts):
             for way in (RIGHT, LEFT):

time: 125 us -> 127 us (1.016)
  no operation moved by 1% of the time
where the time goes in v5:
time: 127 us; the launch traced here: 125 us
  Pallas kernels  119 us (94%)
  local copies, waits for them, and re-layouts  3.4 us (3%)
  other arithmetic  1.91 us (2%)
    pallas_call x1, Pallas kernels, exchange(): pl.pallas_call(functools.partial(exchange_kernel, n, m, share), out_shape...  113 us
    pallas_call x1, Pallas kernels, moment(): pl.pallas_call(functools.partial(moment_kernel, token_total, tile), out_s...  6.26 us
    unnamed x4, local copies, waits for them, and re-layouts  3.17 us

profile of v5, /device:TPU:15, one launch (start us, length us, event | category | flops | bytes accessed | tf_op | source)
XLA Modules:
  0.0 124.7 jit_solution(9813225014355011910)
XLA Ops:
  0.0 0.7 compare_reduce_fusion.1
  0.7 0.1 copy.9
  0.8 0.2 reduce-window.17
  1.0 0.1 add_reduce_fusion
  1.1 0.1 copy.8
  1.2 0.2 reduce-window.16
  1.4 0.1 add_reduce_fusion.1
  1.5 0.6 add_convert_fusion.chooser
  2.2 113.1 %shard_map.55 = (bf16[2,512,1024]{2,1,0:T(8,128)(2,1)}, bf16[2,512,1024]{2,1,0:T(8,128)(2,1)}) custom-call(bf16[2,64,128]{2,1,0:T(8,128)(2,1)} %add_convert_fusion.chooser, bf16[128,4096]{1,0:T(8,128)(2,1)} %tokens.1, bf16[2,128,2048]{2,1,0:T(8,128)(2,1)} %grads.1, bf16[2,512,1024]{2,1,0:T(8,128)(2,1)} %act_basis.1, bf16[2,2048,1024]{2,1,0:T(8,128)(2,1)} %grad_basis.1), custom_call_target="tpu_custom_call" | custom-call | flops 5368709120 | bytes 20971520 | tf_op jit(solution)/shard_map/pallas_call | solution.py:376
  115.3 0.0 copy-start
  115.3 1.6 %copy-done = bf16[2,512,1024]{2,1,0:T(8,128)(2,1)S(1)} copy-done((bf16[2,512,1024]{2,1,0:T(8,128)(2,1)S(1)}, bf16[2,512,1024]{2,1,0:T(8,128)(2,1)}, u32[]{:S(2)}) %copy-start) | copy-done | bytes 2097176
  116.8 0.0 copy-start.1
  116.8 1.6 %copy-done.1 = bf16[2,512,1024]{2,1,0:T(8,128)(2,1)S(1)} copy-done((bf16[2,512,1024]{2,1,0:T(8,128)(2,1)S(1)}, bf16[2,512,1024]{2,1,0:T(8,128)(2,1)}, u32[]{:S(2)}) %copy-start.1) | copy-done | bytes 2097176
  118.4 6.3 %shard_map.56 = f32[2,1024,1024]{2,1,0:T(8,128)} custom-call(bf16[2,512,1024]{2,1,0:T(8,128)(2,1)S(1)} %copy-done.1, bf16[2,512,1024]{2,1,0:T(8,128)(2,1)S(1)} %copy-done), custom_call_target="tpu_custom_call" | custom-call | tf_op jit(solution)/shard_map/pallas_call | solution.py:437
  (3 shorter events, 0.0 us)
Async XLA Ops:
  115.3 1.6 %copy-start = (bf16[2,512,1024]{2,1,0:T(8,128)(2,1)S(1)}, bf16[2,512,1024]{2,1,0:T(8,128)(2,1)}, u32[]{:S(2)}) copy-start(bf16[2,512,1024]{2,1,0:T(8,128)(2,1)} %get-tuple-element.8.act_sq) | copy-start | bytes 6291460
  116.8 1.6 %copy-start.1 = (bf16[2,512,1024]{2,1,0:T(8,128)(2,1)S(1)}, bf16[2,512,1024]{2,1,0:T(8,128)(2,1)}, u32[]{:S(2)}) copy-start(bf16[2,512,1024]{2,1,0:T(8,128)(2,1)} %get-tuple-element.7.grad_sq) | copy-start | bytes 6291460

commit v6 on v5

--- a/solution.py
+++ b/solution.py
@@ -55,7 +55,7 @@
 
 def exchange_kernel(
     n, m, share, chooser, tokens, grads, act_basis, grad_basis, act_sq, grad_sq,
-    picked_act, picked_grad, unscale, sum_out, sum_in, act_w, grad_w, rows_in, part, grad_all, grad_part, grad_in,
+    picked_act, picked_grad, unscale, sum_out, sum_in, act_w, grad_w, rows_in, part, grad_all, grad_part, grad_out, grad_in,
     load_sem, tok_send, tok_recv, share_send, share_recv, sum_send, sum_recv,
     grad_send, grad_recv, act_send, act_recv, part_send, part_recv, sq_send, sq_recv,
 ):
@@ -193,6 +193,7 @@
                 out = jnp.dot(lhs, grad_w[e, :, cols], preferred_element_type=jnp.float32)
                 for i, u in enumerate(at):
                     grad_part[u, :, cols] = out[i * cap : (i + 1) * cap]
+                    grad_out[u, :, cols] = out[i * cap : (i + 1) * cap].astype(jnp.bfloat16)
 
         for i in range(len(units[step])):
             u = first[step] + i
@@ -205,7 +206,7 @@
         q, k = u % m, u // m
         slot = lax.rem(mine - q - 1 + 2 * m, m)
         return remote(
-            grad_part.at[u], grad_in.at[k, slot], part_send.at[u], part_recv.at[k, slot], owner=q
+            grad_out.at[u], grad_in.at[k, slot], part_send.at[u], part_recv.at[k, slot], owner=q
         )
 
     def square_copy(u, step, way, e, j):
@@ -227,7 +228,7 @@
                     pltpu.make_async_copy(
                         grad_in.at[k, slot], grad_in.at[k, slot], part_recv.at[k, slot]
                     ).wait()
-                    total = total + grad_in[k, slot]
+                    total = total + grad_in[k, slot].astype(jnp.float32)
                 grad_sq[e, unit_rows(step, way), :] = jnp.square(total).astype(jnp.bfloat16)
                 for j in range(1, m):
                     square_copy(u, step, way, e, j).start()
@@ -322,12 +323,12 @@
             act_start()
         else:
             gather_step(*act_ring, hop - half)
-        while done < min(half, (2 * hop + 1) // 3):
+        while done < min(half, hop):
             done += 1
             gather_step(*grad_ring, done)
             project(done)
             reduce(done - 1)
-        if hop == 2 * half - 1:
+        if hop == min(half + 2, 2 * half - 1):
             reduce(half)
 
     for step in units:
@@ -393,7 +394,8 @@
             pltpu.VMEM((experts, n * cap, act_columns), jnp.float32),
             pltpu.VMEM((experts, n * cap, window), jnp.bfloat16),
             pltpu.VMEM((count, cap, columns), jnp.float32),
-            pltpu.VMEM((kept, m - 1, cap, columns), jnp.float32),
+            pltpu.VMEM((count, cap, columns), jnp.bfloat16),
+            pltpu.VMEM((kept, m - 1, cap, columns), jnp.bfloat16),
             dma((3,)),
             dma((n,)),
             dma((n,)),

time: 127 us -> 117 us (0.921)
  the two profiles are of different devices: /device:TPU:15 before, /device:TPU:0 now
where the time goes in v6:
time: 117 us
  Pallas kernels  111 us (95%)
  local copies, waits for them, and re-layouts  3.4 us (3%)
  other arithmetic  1.91 us (2%)
    pallas_call x1, Pallas kernels, exchange(): pl.pallas_call(functools.partial(exchange_kernel, n, m, share), out_shape...  105 us
    pallas_call x1, Pallas kernels, moment(): pl.pallas_call(functools.partial(moment_kernel, token_total, tile), out_s...  6.26 us
    unnamed x4, local copies, waits for them, and re-layouts  3.17 us

profile of v6, /device:TPU:0, one launch (start us, length us, event | category | flops | bytes accessed | tf_op | source)
XLA Modules:
  0.0 116.6 jit_solution(16468613912284841028)
XLA Ops:
  0.0 0.7 compare_reduce_fusion.1
  0.7 0.1 copy.9
  0.8 0.2 reduce-window.17
  1.0 0.1 add_reduce_fusion
  1.1 0.1 copy.8
  1.2 0.2 reduce-window.16
  1.4 0.1 add_reduce_fusion.1
  1.5 0.6 add_convert_fusion.chooser
  2.2 105.0 %shard_map.55 = (bf16[2,512,1024]{2,1,0:T(8,128)(2,1)}, bf16[2,512,1024]{2,1,0:T(8,128)(2,1)}) custom-call(bf16[2,64,128]{2,1,0:T(8,128)(2,1)} %add_convert_fusion.chooser, bf16[128,4096]{1,0:T(8,128)(2,1)} %tokens.1, bf16[2,128,2048]{2,1,0:T(8,128)(2,1)} %grads.1, bf16[2,512,1024]{2,1,0:T(8,128)(2,1)} %act_basis.1, bf16[2,2048,1024]{2,1,0:T(8,128)(2,1)} %grad_basis.1), custom_call_target="tpu_custom_call" | custom-call | flops 5368709120 | bytes 20971520 | tf_op jit(solution)/shard_map/pallas_call | solution.py:377
  107.1 0.0 copy-start
  107.1 1.6 %copy-done = bf16[2,512,1024]{2,1,0:T(8,128)(2,1)S(1)} copy-done((bf16[2,512,1024]{2,1,0:T(8,128)(2,1)S(1)}, bf16[2,512,1024]{2,1,0:T(8,128)(2,1)}, u32[]{:S(2)}) %copy-start) | copy-done | bytes 2097176
  108.7 0.0 copy-start.1
  108.7 1.6 %copy-done.1 = bf16[2,512,1024]{2,1,0:T(8,128)(2,1)S(1)} copy-done((bf16[2,512,1024]{2,1,0:T(8,128)(2,1)S(1)}, bf16[2,512,1024]{2,1,0:T(8,128)(2,1)}, u32[]{:S(2)}) %copy-start.1) | copy-done | bytes 2097176
  110.3 6.3 %shard_map.56 = f32[2,1024,1024]{2,1,0:T(8,128)} custom-call(bf16[2,512,1024]{2,1,0:T(8,128)(2,1)S(1)} %copy-done.1, bf16[2,512,1024]{2,1,0:T(8,128)(2,1)S(1)} %copy-done), custom_call_target="tpu_custom_call" | custom-call | tf_op jit(solution)/shard_map/pallas_call | solution.py:439
  (3 shorter events, 0.0 us)
Async XLA Ops:
  107.1 1.6 %copy-start = (bf16[2,512,1024]{2,1,0:T(8,128)(2,1)S(1)}, bf16[2,512,1024]{2,1,0:T(8,128)(2,1)}, u32[]{:S(2)}) copy-start(bf16[2,512,1024]{2,1,0:T(8,128)(2,1)} %get-tuple-element.8.act_sq) | copy-start | bytes 6291460
  108.7 1.6 %copy-start.1 = (bf16[2,512,1024]{2,1,0:T(8,128)(2,1)S(1)}, bf16[2,512,1024]{2,1,0:T(8,128)(2,1)}, u32[]{:S(2)}) copy-start(bf16[2,512,1024]{2,1,0:T(8,128)(2,1)} %get-tuple-element.7.grad_sq) | copy-start | bytes 6291460
